TPU v7x, 128 devices: a whole 4x4x4 slice. The times are simulated.
128 devices in a mesh: slot: 16 (over z, x_hi, core), tok: 8 (over y, x_lo).
Axes of the slice: x: 4 (x_hi: 2, x_lo: 2; x = x_hi * 2 + x_lo), y: 4, z: 4, core: 2. Of those that a mesh axis runs over, the one named last changes fastest.
Arguments:
- latents: bfloat16 [16, 1024, 5120], P('slot', 'tok'), may hold values from -3 to 3
- gain: float32 [5120], replicated, may hold values from 0.5 to 1.5
- mod_table: float32 [16, 2, 5120], replicated, may hold values from -3 to 3
- slot_noise_level: int32 [16], P('slot'), may hold values from 0 to 15
- key_block_index: int32 [16, 8, 4], P('slot'), may hold values from 0 to 15
- counts: int32 [16, 8], P('slot'), may hold values from 1 to 4
- w_qkv: bfloat16 [3, 5120, 3072], P(None, 'slot', 'tok')
- w_out: bfloat16 [3072, 5120], P('tok', 'slot'), may hold values from -0.25 to 0.25
Outputs:
- shifted: bfloat16 [16, 1024, 5120], P('slot', 'tok')
Inputs may be any that keep to these rules, and one draw needn't show every extreme that they name: `key_block_index`: entries 0 to 7 name the slot's own tiles, 8 to 15 the preceding slot's; only the first counts entries of a list are read, and they may repeat.
All inputs are finite; a program needn't handle non-finite values.
Results may differ from a plain program's by a relative error of at most 0.018.
Values may be sent and summed in bfloat16 or wider, within the bound.
A program may use at most 128 MiB of HBM per device.

v0:
```python
import math

import jax
import jax.numpy as jnp
from jax import lax
from jax.sharding import PartitionSpec as P

HD = 128
BLK = 128
LISTED_BLOCKS = 4


def shifted(value, axis, by):
    size = lax.axis_size(axis)
    return lax.ppermute(value, axis, [(i, (i + by) % size) for i in range(size)])


def tile_allowed(ids, count):
    tiles = ids.shape[0]
    valid = jnp.arange(LISTED_BLOCKS, dtype=jnp.int32)[None, :] < count[:, None]
    hit = (ids[:, :, None] == jnp.arange(2 * tiles, dtype=jnp.int32)[None, None, :]) & valid[
        :, :, None
    ]
    hit = jnp.any(hit, axis=1)
    return jnp.repeat(jnp.repeat(hit, BLK, axis=0), BLK, axis=1)


def attend(queries, keys, value_rows, allowed):
    rows = queries.shape[0]
    heads = queries.shape[1] // HD
    qh = queries.reshape(rows, heads, HD).transpose(1, 0, 2)
    kh = keys.reshape(keys.shape[0], heads, HD).transpose(1, 0, 2)
    vh = value_rows.reshape(value_rows.shape[0], heads, HD).transpose(1, 0, 2)

    def one_head(items):
        query, key, value = items
        scores = jnp.einsum("qd,kd->qk", query, key, preferred_element_type=jnp.float32) * (
            1.0 / math.sqrt(HD)
        )
        scores = jnp.where(allowed, scores, -1e30)
        top = jnp.max(scores, axis=1, keepdims=True)
        expo = jnp.exp(scores - top)
        probs = (expo / jnp.sum(expo, axis=1, keepdims=True)).astype(jnp.bfloat16)
        return jnp.dot(probs, value, preferred_element_type=jnp.float32).astype(jnp.bfloat16)

    out = lax.map(one_head, (qh, kh, vh))
    return out.transpose(1, 0, 2).reshape(rows, heads * HD)


def body(latents, gain, mod_table, slot_noise_level, key_block_index, counts, w_qkv, w_out):
    tokens = latents[0]
    levels = mod_table.shape[0]
    pick = (jnp.arange(levels, dtype=jnp.int32) == slot_noise_level[0])[:, None, None]
    modul = jnp.sum(jnp.where(pick, mod_table, 0.0), axis=0)
    xf = tokens.astype(jnp.float32)
    mean = jnp.mean(xf, axis=-1, keepdims=True)
    centred = xf - mean
    var = jnp.mean(centred * centred, axis=-1, keepdims=True)
    gaussian_sample = centred * lax.rsqrt(var + 1e-06)
    normed = (gaussian_sample * gain * (1.0 + modul[0]) + modul[1]).astype(jnp.bfloat16)
    prev = shifted(normed, "slot", 1)
    own_rows, prev_rows = (
        lax.all_gather(normed, "tok", axis=0, tiled=True),
        lax.all_gather(prev, "tok", axis=0, tiled=True),
    )
    piece = lax.all_gather(w_qkv, "slot", axis=1, tiled=True)
    own_acc = jnp.einsum("tr,jrc->jtc", own_rows, piece, preferred_element_type=jnp.float32)
    prev_acc = jnp.einsum("tr,jrc->jtc", prev_rows, piece[1:], preferred_element_type=jnp.float32)
    own_proj = own_acc
    prev_proj = prev_acc
    own_proj = own_proj.astype(jnp.bfloat16)
    prev_proj = prev_proj.astype(jnp.bfloat16)
    keys_prev = prev_proj[0]
    values_prev = prev_proj[1]
    ctx_keys = jnp.concatenate([own_proj[1], keys_prev], axis=0)
    ctx_values = jnp.concatenate([own_proj[2], values_prev], axis=0)
    allowed = tile_allowed(key_block_index[0], counts[0])
    attn = attend(own_proj[0], ctx_keys, ctx_values, allowed)
    attn_use, tokens_use = (attn, tokens)
    terms = jnp.dot(
        attn_use,
        lax.all_gather(w_out, "slot", axis=1, tiled=True),
        preferred_element_type=jnp.float32,
    )
    summed = lax.psum_scatter(
        terms.astype(jnp.bfloat16), "tok", scatter_dimension=0, tiled=True
    ).astype(jnp.float32)
    updated = (tokens_use.astype(jnp.float32) + summed).astype(jnp.bfloat16)
    updated = shifted(updated, "slot", 1)
    return updated[None]


def solution(mesh):
    in_specs = (
        P("slot", "tok", None),
        P(),
        P(),
        P("slot"),
        P("slot", None, None),
        P("slot", None),
        P(None, "slot", "tok"),
        P("tok", "slot"),
    )
    out_specs = P("slot", "tok", None)
    return jax.shard_map(body, mesh=mesh, in_specs=in_specs, out_specs=out_specs, check_vma=False)
```

profile of v0, /device:TPU:1, one launch (start us, length us, event | category | flops | bytes accessed | tf_op | source)
XLA Modules:
  0.0 846.7 jit_solution(5007894140447140117)
XLA Ops:
  6.5 0.0 copy-start
  6.5 0.0 all-gather.5.cloned.1.call-start
  7.3 1.5 select_reduce_fusion
  8.8 1.6 convert_reduce_fusion
  10.4 0.0 copy-done
  10.4 0.5 fusion.23
  10.9 0.0 copy-done.3
  10.9 0.0 copy-start.5
  10.9 0.0 copy-start.4
  10.9 1.7 fusion.27
  12.6 0.0 all-gather.5.cloned.1.call-update
  12.7 0.0 all-gather.7.cloned.1.call-start
  12.7 0.7 all-gather.7.cloned.1.call-update
  13.4 0.0 all-gather.9.cloned.1.call-start
  13.5 4.2 collective-permute-start
  17.7 30.3 %collective-permute-done = bf16[128,5120]{1,0:T(8,128)(2,1)S(1)} collective-permute-done((bf16[128,5120]{1,0:T(8,128)(2,1)}, bf16[128,5120]{1,0:T(8,128)(2,1)S(1)}, u32[]{:S(2)}, u32[]{:S(2)}) %collective-permute-start) | collective-permute-done | bytes 1310752 | tf_op jit(solution)/shard_map/ppermute | solution.py:15
  48.0 1.1 copy-done.2
  49.1 0.0 all-gather.9.cloned.1.call-update
  49.1 0.0 all-gather.11.cloned.1.call-start
  49.2 0.5 all-gather.11.cloned.1.call-update
  49.7 0.2 reduce-scatter.2.cloned.1.call-start
  49.9 0.0 copy-done.5
  50.0 0.0 copy-done.4
  50.0 0.1 fusion.42
  50.1 180.5 %all-gather.5.cloned.1.call-done = bf16[1024,5120]{1,0:T(8,128)(2,1)} async-done(((bf16[128,5120]{1,0:T(8,128)(2,1)}), bf16[1024,5120]{1,0:T(8,128)(2,1)}) %all-gather.5.cloned.1.call-update) | async-done | bytes 10485776 | tf_op jit(solution)/shard_map/all_gather | solution.py:63
  230.6 92.6 %all-gather.7.cloned.1.call-done = bf16[3,5120,384]{2,1,0:T(8,128)(2,1)} async-done(((bf16[3,320,384]{2,1,0:T(8,128)(2,1)}), bf16[3,5120,384]{2,1,0:T(8,128)(2,1)}) %all-gather.7.cloned.1.call-update) | async-done | bytes 11796496 | tf_op jit(solution)/shard_map/all_gather | solution.py:66
  323.2 18.0 %convert_bitcast_fusion.1 = bf16[3,1024,384]{1,2,0:T(8,128)(2,1)S(1)} fusion(bf16[3,5120,384]{2,1,0:T(8,128)(2,1)} %all-gather.7.cloned.1.call-done, bf16[1024,5120]{1,0:T(8,128)(2,1)} %all-gather.5.cloned.1.call-done), kind=kOutput, calls=%fused_computation.35 | convolution fusion | flops 12080775168 | bytes 24641536 | tf_op jit(solution)/shard_map/tr,jrc->jtc/dot_general | solution.py:67
  341.2 0.2 fusion.44
  341.4 188.3 %all-gather.9.cloned.1.call-done = bf16[1024,5120]{1,0:T(8,128)(2,1)} async-done(((bf16[128,5120]{1,0:T(8,128)(2,1)}), bf16[1024,5120]{1,0:T(8,128)(2,1)}) %all-gather.9.cloned.1.call-update) | async-done | bytes 10485776 | tf_op jit(solution)/shard_map/all_gather | solution.py:64
  529.7 13.4 %fusion.36 = bf16[2,1024,384]{1,2,0:T(8,128)(2,1)S(1)} fusion(bf16[3,5120,384]{2,1,0:T(8,128)(2,1)} %all-gather.7.cloned.1.call-done, bf16[1024,5120]{1,0:T(8,128)(2,1)} %all-gather.9.cloned.1.call-done), kind=kOutput, calls=%fused_computation.39 | convolution fusion | flops 8053850112 | bytes 19922944 | tf_op jit(solution)/shard_map/tr,jrc->jtc/dot_general | solution.py:68
  543.2 1.3 fusion.45
  544.5 0.4 copy.26
  544.9 0.4 copy.28
  545.2 1.5 copy.27
  546.8 2.3 copy.29
  549.1 1.2 copy.24
  550.2 3.0 maximum_bitcast_fusion
  553.3 46.3 %while.11 = (s32[]{:T(128)}, bf16[3,1024,128]{1,2,0:T(8,128)(2,1)}, bf16[3,1024,128]{2,1,0:T(8,128)(2,1)}, bf16[3,2048,128]{2,1,0:T(8,128)(2,1)}, bf16[3,2048,12...) while((s32[]{:T(128)}, bf16[3,1024,128]{1,2,0:T(8,128)(2,1)}, ...), condition=%wide.region_7.8_spmd.clone, body=%wide.region_4.7_spmd.clone.sunk | while | flops 1090648064 | bytes 32020556 | solution.py:46
  553.5 6.9 broadcast_in_dim.58
  560.4 3.3 fusion.54
  563.7 1.3 fusion.55
  565.0 3.0 fusion.56
  568.0 0.1 copy.37
  568.2 0.7 constant_dynamic-update-slice_fusion.2
  568.9 6.9 broadcast_in_dim.58
  575.8 3.3 fusion.54
  579.1 1.3 fusion.55
  580.4 3.0 fusion.56
  583.4 0.1 copy.37
  583.5 0.7 constant_dynamic-update-slice_fusion.2
  584.2 6.9 broadcast_in_dim.58
  591.1 3.3 fusion.54
  594.4 1.3 fusion.55
  595.7 3.0 fusion.56
  598.7 0.1 copy.37
  598.8 0.7 constant_dynamic-update-slice_fusion.2
  599.6 10.5 %convolution_convert_fusion = bf16[1024,5120]{1,0:T(8,128)(2,1)} fusion(bf16[1024,384]{0,1:T(8,128)(2,1)} %bitcast.102, bf16[384,5120]{0,1:T(8,128)(2,1)} %all-gather.11.cloned.1.call-done), kind=kOutput, calls=%fused_computation.21 | convolution fusion | flops 4031774720 | bytes 15204352 | tf_op jit(solution)/shard_map/dot_general | solution.py:80
  610.1 0.0 reduce-scatter.2.cloned.1.call-update
  610.1 209.8 %reduce-scatter.2.cloned.1.call-done = bf16[128,5120]{1,0:T(8,128)(2,1)} async-done(((bf16[1024,5120]{1,0:T(8,128)(2,1)}), bf16[128,5120]{1,0:T(8,128)(2,1)}) %reduce-scatter.2.cloned.1.call-update) | async-done | bytes 1310736 | tf_op jit(solution)/shard_map/reduce_scatter | solution.py:85
  819.9 0.0 copy-done.1
  819.9 1.6 fusion.28
  821.6 3.0 collective-permute-start.1
  824.6 14.6 %collective-permute-done.1 = bf16[128,5120]{1,0:T(8,128)(2,1)S(1)} collective-permute-done((bf16[128,5120]{1,0:T(8,128)(2,1)S(1)}, bf16[128,5120]{1,0:T(8,128)(2,1)S(1)}, u32[]{:S(2)}, u32[]{:S(2)}) %collective-permute-start.1) | collective-permute-done | bytes 1310752 | tf_op jit(solution)/shard_map/ppermute | solution.py:15
  839.1 1.1 copy.49
  (11 shorter events, 0.1 us)
Async XLA Ops:
  6.5 3.9 copy-start
  6.5 4.4 copy-start.3
  6.5 224.1 %all-gather.5.cloned.1.call-start = ((), (), s32[]{:S(2)}) async-start(), calls=%async_computation.1 | async-start | bytes 11796480 | tf_op jit(solution)/shard_map/all_gather | solution.py:63
  10.9 39.0 %copy-start.5 = (s32[1,8]{1,0:T(1,128)S(1)}, s32[1,8]{1,0:T(1,128)}, u32[]{:S(2)}) copy-start(s32[1,8]{1,0:T(1,128)} %param.15) | copy-start | bytes 100
  10.9 39.0 %copy-start.4 = (s32[1,8,4]{1,2,0:T(4,128)S(1)}, s32[1,8,4]{1,2,0:T(4,128)}, u32[]{:S(2)}) copy-start(s32[1,8,4]{1,2,0:T(4,128)} %param.14) | copy-start | bytes 388
  12.7 310.5 %all-gather.7.cloned.1.call-start = ((), (), s32[]{:S(2)}) async-start(), calls=%async_computation.2 | async-start | bytes 12533760 | tf_op jit(solution)/shard_map/all_gather | solution.py:66
  13.4 516.3 %all-gather.9.cloned.1.call-start = ((), (), s32[]{:S(2)}) async-start(), calls=%async_computation.3 | async-start | bytes 11796480 | tf_op jit(solution)/shard_map/all_gather | solution.py:64
  13.5 34.5 %collective-permute-start = (bf16[128,5120]{1,0:T(8,128)(2,1)}, bf16[128,5120]{1,0:T(8,128)(2,1)S(1)}, u32[]{:S(2)}, u32[]{:S(2)}) collective-permute-start(bf16[128,5120]{1,0:T(8,128)(2,1)} %fusion.27), channel_id=1, source_target_pairs={{0,8},{8,16},{16,24},{24,32},{32,40},{40,48},{48,56},{56,64},{64,7... | collective-permute-start | bytes 3932168 | tf_op jit(solution)/shard_map/ppermute | solution.py:15
  48.0 1.1 copy-start.2
  49.1 550.5 %all-gather.11.cloned.1.call-start = ((), (), s32[]{:S(2)}) async-start(), calls=%async_computation.4 | async-start | bytes 4177920 | tf_op jit(solution)/shard_map/all_gather | solution.py:82
  49.7 770.2 %reduce-scatter.2.cloned.1.call-start = ((), (), s32[]{:S(2)}) async-start(), calls=%async_computation.5 | async-start | bytes 11796480 | tf_op jit(solution)/shard_map/reduce_scatter | solution.py:85
  610.1 209.9 %copy-start.1 = (bf16[1,128,5120]{2,1,0:T(8,128)(2,1)S(1)}, bf16[1,128,5120]{2,1,0:T(8,128)(2,1)}, u32[]{:S(2)}) copy-start(bf16[1,128,5120]{2,1,0:T(8,128)(2,1)} %param.10) | copy-start | bytes 3932164
  821.6 17.5 %collective-permute-start.1 = (bf16[128,5120]{1,0:T(8,128)(2,1)S(1)}, bf16[128,5120]{1,0:T(8,128)(2,1)S(1)}, u32[]{:S(2)}, u32[]{:S(2)}) collective-permute-start(bf16[128,5120]{1,0:T(8,128)(2,1)S(1)} %fusion.28), channel_id=1, source_target_pairs={{0,8},{8,16},{16,24},{24,32},{32,40},{40,48},{48,56},{56,64},{64,7... | collective-permute-start | bytes 3932168 | tf_op jit(solution)/shard_map/ppermute | solution.py:15
Sparse Core Ops, SparseCore 0:
  12.8 217.7 all-gather.4
  233.1 90.0 all-gather.6
  324.8 204.8 all-gather.8
  532.1 55.6 all-gather.10
  610.2 209.6 reduce-scatter.1
where the time goes:
time: 850 us; the launch traced here: 847 us
  waiting for transfers between devices  717 us (84%)
  matrix products  60.8 us (7%)
  local copies, waits for them, and re-layouts  32.8 us (4%)
  between operations  14 us (2%)
  other arithmetic  13.8 us (2%)
    reduce_scatter x1, waiting for transfers between devices, body(): lax.psum_scatter(terms.astype(jnp.bfloat16), 'tok', scatter_dimension=0,...  210 us
    all_gather x1, waiting for transfers between devices, body(): lax.all_gather(prev, 'tok', axis=0, tiled=True)  188 us
    all_gather x1, waiting for transfers between devices, body(): lax.all_gather(normed, 'tok', axis=0, tiled=True)  181 us
    all_gather x1, waiting for transfers between devices, body(): piece = lax.all_gather(w_qkv, 'slot', axis=1, tiled=True)  92.6 us
    ppermute x2, waiting for transfers between devices, shifted(): lax.ppermute(value, axis, [(i, (i + by) % size) for i in range(size)])  44.9 us
    broadcast_in_dim x4, local copies, waits for them, and re-layouts, tile_allowed(): return jnp.repeat(jnp.repeat(hit, BLK, axis=0), BLK, axis=1)  20.7 us
    dot_general x1, matrix products, body(): jnp.einsum('tr,jrc->jtc', own_rows, piece, preferred_element_type=jnp.flo...  18 us
  transfers between devices with their start and end apart: 7, of which 6 were waited for; matrix products, arithmetic and copies ran while one was open for 10% of the time, Pallas kernels for 0%

commit v1 on v0

v1 whole, which is shorter than its diff:
```python
import functools
import math

import jax
import jax.numpy as jnp
from jax import lax
from jax.experimental import pallas as pl
from jax.experimental.pallas import tpu as pltpu
from jax.sharding import PartitionSpec as P

MESH = pl.DeviceIdType.MESH
BF16 = jnp.bfloat16
F32 = jnp.float32

HD = 128
ROWS = 128
D = 5120
QKV = 1152
PIECE = 320
HALF = 64
KCHUNK = 1024
GROUP = 384

NAMES = (
    "w_xh", "w_zp0", "w_zm0", "w_co0", "w_zp1", "w_zm1", "w_co1", "w_fp0", "w_fm0", "w_co2", "w_co3",
    "w_fp1", "w_fm1", "w_co4", "w_co5", "w_co6", "w_co7", "t_x0", "t_x1", "t_yp0", "t_yp1", "t_ym0", "t_ym1",
    "t_fp", "t_fm", "u_yp0", "u_yp1", "u_ym0", "u_ym1", "u_x0", "u_x1", "o_a0", "o_a1", "o_a2", "o_a3",
    "o_xh", "o_zp", "o_zm", "o_co0", "o_fp", "o_fm", "o_co1", "o_co2", "o_co3",
)
SEM = {name: i for i, name in enumerate(NAMES)}
KV0 = len(NAMES)
A_YP = KV0 + 8
A_YM = A_YP + 8
A_FP = A_YM + 8
A_FM = A_FP + 8
P_X = A_FM + 8
S_Y = P_X + 4
OUT = S_Y + 4
N_SEM = OUT + 4


def kernel(lat, gain, mod, level, ids, counts, wq, wo, out,
           x, w, wout, q, ctx, att, acc, psend, precv, ssend, srecv, upd, latc, local, ss, rs):
    s, t = lax.axis_index("slot"), lax.axis_index("tok")
    z, h, c = s // 4, (s // 2) % 2, s % 2
    y, l = t // 2, t % 2

    def slot(zz, hh, cc):
        return (zz % 4) * 4 + hh * 2 + cc

    def tok(yy, ll):
        return (yy % 4) * 2 + ll

    XL = (s, tok(y, 1 - l))
    YP, YM, Y2 = (s, tok(y + 1, l)), (s, tok(y + 3, l)), (s, tok(y + 2, l))
    ZP, ZM = (slot(z + 1, h, c), t), (slot(z + 3, h, c), t)
    XH, CO = (slot(z, 1 - h, c), t), (slot(z, h, 1 - c), t)
    NX, PV = ((s + 1) % 16, t), ((s + 15) % 16, t)

    def copy(src, dst, sem, dev):
        k = SEM[sem] if isinstance(sem, str) else sem
        return pltpu.make_async_remote_copy(
            src_ref=src, dst_ref=dst, send_sem=ss.at[k], recv_sem=rs.at[k], device_id=dev, device_id_type=MESH
        )

    sent = []

    def send(ref, sem, dev):
        cp = copy(ref, ref, sem, dev)
        cp.start()
        sent.append(cp)
        return cp

    barrier = pltpu.get_barrier_semaphore()
    peers = (XL, YP, YM, Y2, ZP, ZM, XH, CO, NX, PV)
    for dev in peers:
        pl.semaphore_signal(barrier, inc=1, device_id=dev, device_id_type=MESH)

    def wrows(piece, first=0, size=PIECE):
        return w.at[pl.ds(pl.multiple_of(piece * PIECE + first, 32), size)]

    own = [
        pltpu.make_async_copy(
            wq.at[j], w.at[pl.ds(pl.multiple_of(s * PIECE, 64), PIECE), pl.ds(j * GROUP, GROUP)], local.at[j]
        )
        for j in range(3)
    ]
    for cp in own:
        cp.start()
    for cp in own:
        cp.wait()
    pl.semaphore_wait(barrier, len(peers))

    mine = wrows(s)
    w_xh = send(mine, "w_xh", XH)
    w_zp0 = send(mine, "w_zp0", ZP)
    w_zm0 = send(mine, "w_zm0", ZM)
    w_co = [send(mine, "w_co0", CO)]

    lv = level[0]
    factor = gain[...] * (1.0 + mod[lv, 0:1, :])
    offset = mod[lv, 1:2, :]

    def norm(i, _):
        rows = pl.ds(pl.multiple_of(i * 16, 16), 16)
        xf = lat[rows, :].astype(F32)
        mean = jnp.mean(xf, axis=-1, keepdims=True)
        centred = xf - mean
        var = jnp.mean(centred * centred, axis=-1, keepdims=True)
        x[t, rows, :] = (centred * lax.rsqrt(var + 1e-06) * factor + offset).astype(BF16)
        return 0

    def shard(tt, half):
        return x.at[tt, pl.ds(half * HALF, HALF)]

    t_x, t_yp, t_ym = [], [], []
    for half in range(2):
        lax.fori_loop(half * 4, half * 4 + 4, norm, 0)
        t_yp.append(send(shard(t, half), "t_yp%d" % half, YP))
        t_ym.append(send(shard(t, half), "t_ym%d" % half, YM))
        t_x.append(send(shard(t, half), "t_x%d" % half, XL))

    yd = h * 2 + c
    gather = y == yd
    active = c == y % 2
    relay = active & (h != y // 2)

    def orows(zz, first, size):
        return wout.at[zz % 4, pl.ds(first, size)]

    def o_first():
        dst = wout.at[z, pl.ds(pl.multiple_of(y * GROUP, 128), GROUP)]
        return copy(wo, dst, SEM["o_a0"] + (y - yd + 4) % 4, (s, tok(yd, l)))

    def o_copy(name, dev):
        zz = {"o_xh": z, "o_zp": z, "o_zm": z, "o_co0": z, "o_fp": z + 3, "o_fm": z + 1, "o_co1": z + 3, "o_co2": z + 1, "o_co3": z + 2}[name]
        if name == "o_fp":
            ref = orows(zz, 0, 768)
        elif name == "o_fm":
            ref = orows(zz, 768, 768)
        else:
            ref = wout.at[zz % 4]
        return copy(ref, ref, name, dev)

    @pl.when(jnp.logical_not(gather))
    def _():
        o_first().start()

    @pl.when(gather)
    def _():
        cp = pltpu.make_async_copy(wo, wout.at[z, pl.ds(pl.multiple_of(y * GROUP, 128), GROUP)], local.at[3])
        cp.start()
        cp.wait()

    for yy in range(4):
        for zz in range(4):
            first = (zz * 4 + yy) * PIECE
            latc[yy, zz] = lat[:, first:first + PIECE]

    tm, tp, tx = tok(y + 3, l), tok(y + 1, l), tok(y, 1 - l)
    t2 = tok(y + 2, l)
    w_xh.wait_recv()
    px = slot(z, 1 - h, c)
    w_zp1 = send(wrows(px), "w_zp1", ZP)
    w_zm1 = send(wrows(px), "w_zm1", ZM)
    w_co.append(send(wrows(px), "w_co1", CO))

    t_yp[0].wait_recv()
    t_fp = send(shard(tm, 0), "t_fp", YP)
    w_zp0.wait_recv()
    pm = slot(z + 3, h, c)
    w_fp0 = send(wrows(pm, 0, PIECE // 2), "w_fp0", ZP)
    w_co.append(send(wrows(pm), "w_co2", CO))
    w_zm0.wait_recv()
    pp = slot(z + 1, h, c)
    w_fm0 = send(wrows(pp, PIECE // 2, PIECE // 2), "w_fm0", ZM)
    w_co.append(send(wrows(pp), "w_co3", CO))
    t_ym[1].wait_recv()
    t_fm = send(shard(tp, 1), "t_fm", YM)

    u_yp, u_ym = [], []
    for half in range(2):
        t_x[half].wait_recv()
        u_yp.append(send(shard(tx, half), "u_yp%d" % half, YP))
        u_ym.append(send(shard(tx, half), "u_ym%d" % half, YM))

    @pl.when(gather)
    def _():
        for d in range(1, 4):
            src = wout.at[z, pl.ds(0, GROUP)]
            copy(src, src, SEM["o_a0"] + d, YP).wait_recv()
        o_copy("o_xh", XH).start()

    w_zp1.wait_recv()
    pm1 = slot(z + 3, 1 - h, c)
    w_fp1 = send(wrows(pm1, 0, PIECE // 2), "w_fp1", ZP)
    w_co.append(send(wrows(pm1), "w_co4", CO))
    w_zm1.wait_recv()
    pp1 = slot(z + 1, 1 - h, c)
    w_fm1 = send(wrows(pp1, PIECE // 2, PIECE // 2), "w_fm1", ZM)
    w_co.append(send(wrows(pp1), "w_co5", CO))

    @pl.when(relay)
    def _():
        o_copy("o_xh", XH).wait_recv()

    @pl.when(active)
    def _():
        o_copy("o_zp", ZP).start()
        o_copy("o_zm", ZM).start()
        o_copy("o_co0", CO).start()

    w_fp0.wait_recv()
    w_fm0.wait_recv()
    w_co.append(send(wrows(slot(z + 2, h, c)), "w_co6", CO))
    t_fp.wait_recv()
    u_x = [send(shard(t2, 0), "u_x0", XL)]
    t_fm.wait_recv()
    u_x.append(send(shard(t2, 1), "u_x1", XL))
    w_fp1.wait_recv()
    w_fm1.wait_recv()
    w_co.append(send(wrows(slot(z + 2, 1 - h, c)), "w_co7", CO))
    for cp in w_co:
        cp.wait_recv()

    kv = {}

    def project(ta, tb, first):
        def step(k, _):
            cols = pl.ds(pl.multiple_of(k * KCHUNK, KCHUNK), KCHUNK)
            rows = jnp.concatenate([x[ta, :, cols], x[tb, :, cols]], axis=0)
            part = jnp.dot(rows, w[cols, :], preferred_element_type=F32)

            @pl.when(k == 0)
            def _():
                acc[...] = part

            @pl.when(k > 0)
            def _():
                acc[...] += part

            return 0

        lax.fori_loop(0, D // KCHUNK, step, 0)
        for i, tt in enumerate((ta, tb)):
            rows = pl.ds(i * ROWS, ROWS)
            ctx[tt] = acc[rows, GROUP:].astype(BF16)
            cp = copy(ctx.at[tt], ctx.at[8 + tt], KV0 + first + i, NX)
            cp.start()
            kv[first + i] = cp
            sent.append(cp)
            q[tt] = acc[rows, :GROUP].astype(BF16)

    project(t, tx, 0)
    t_yp[1].wait_recv()
    t_ym[0].wait_recv()
    project(tm, tp, 2)

    @pl.when(active)
    def _():
        o_copy("o_zp", ZP).wait_recv()
        o_copy("o_fp", ZP).start()
        o_copy("o_co1", CO).start()
        o_copy("o_zm", ZM).wait_recv()
        o_copy("o_fm", ZM).start()
        o_copy("o_co2", CO).start()

    for half in range(2):
        u_yp[half].wait_recv()
        u_ym[half].wait_recv()
    project(tok(y + 3, 1 - l), tok(y + 1, 1 - l), 4)
    u_x[0].wait_recv()
    u_x[1].wait_recv()
    project(t2, tok(y + 2, 1 - l), 6)

    @pl.when(active)
    def _():
        o_copy("o_fp", ZP).wait_recv()
        o_copy("o_fm", ZM).wait_recv()
        o_copy("o_co3", CO).start()

    for k in range(8):
        kv[k].wait_recv()

    scale = 1.0 / math.sqrt(HD)
    ycols = pl.ds(pl.multiple_of(y * GROUP, 128), GROUP)

    def tile_of(k):
        return 2 * (k % 4) + jnp.where(k < 4, 1 - l, l)

    def acols(yy):
        return pl.ds(pl.multiple_of((yy % 4) * GROUP, 128), GROUP)

    def a_copy(k, base):
        i = tile_of(k)
        if base == A_YP:
            ref, dev = att.at[i, :, ycols], YP
        elif base == A_YM:
            ref, dev = att.at[i, :, ycols], YM
        elif base == A_FP:
            ref, dev = att.at[i, pl.ds(0, HALF), acols(y + 3)], YP
        else:
            ref, dev = att.at[i, pl.ds(HALF, HALF), acols(y + 1)], YM
        return copy(ref, ref, base + k, dev)

    def attend(k):
        i = tile_of(k)
        listed = [ids[i, j] for j in range(4)]
        valid = []
        for j in range(4):
            ok = j < counts[i]
            for e in range(j):
                ok = ok & (listed[e] != listed[j])
            valid.append(ok)
        outs = []
        for head in range(3):
            hc = slice(head * HD, (head + 1) * HD)
            vc = slice(GROUP + head * HD, GROUP + (head + 1) * HD)
            query = q[i, :, hc]
            scores = []
            for j in range(4):
                sc = lax.dot_general(
                    query, ctx[listed[j], :, hc], (((1,), (1,)), ((), ())), preferred_element_type=F32
                ) * scale
                scores.append(jnp.where(valid[j], sc, -1e30))
            top = jnp.maximum(jnp.maximum(scores[0], scores[1]), jnp.maximum(scores[2], scores[3]))
            top = jnp.max(top, axis=1, keepdims=True)
            expo = [jnp.exp(sc - top) for sc in scores]
            total = jnp.sum((expo[0] + expo[1]) + (expo[2] + expo[3]), axis=1, keepdims=True)
            probs = jnp.concatenate([(e / total).astype(BF16) for e in expo], axis=1)
            values = jnp.concatenate([ctx[listed[j], :, vc] for j in range(4)], axis=0)
            outs.append(jnp.dot(probs, values, preferred_element_type=F32).astype(BF16))
        att[i, :, ycols] = jnp.concatenate(outs, axis=1)
        a_copy(k, A_YP).start()
        a_copy(k, A_YM).start()

    def forward(k):
        a_copy(k, A_YP).wait_recv()
        a_copy(k, A_FP).start()
        a_copy(k, A_YM).wait_recv()
        a_copy(k, A_FM).start()

    def product(k, zz):
        return jnp.dot(att[tile_of(k)], wout[zz], preferred_element_type=F32)

    def p_copy(k):
        return copy(psend.at[k], precv.at[k], P_X + k, XL)

    def foreign(k):
        a_copy(k, A_FP).wait_recv()
        a_copy(k, A_FM).wait_recv()
        for zz in range(4):
            psend[k, zz] = product(k, zz).astype(BF16)
        p_copy(k).start()

    def s_copy(yt):
        return copy(ssend.at[yt], srecv.at[y], S_Y + (yt - y + 4) % 4, (s, tok(yt, l)))

    def finish(yt):
        k = yt + 4
        a_copy(k, A_FP).wait_recv()
        a_copy(k, A_FM).wait_recv()
        p_copy(yt).wait_recv()
        for zz in range(4):
            ssend[yt, zz] = (product(k, zz) + precv[yt, zz].astype(F32)).astype(BF16)

        @pl.when(yt != y)
        def _():
            s_copy(yt).start()

        @pl.when(yt == y)
        def _():
            srecv[y] = ssend[yt]

    def wait_out_weights():
        @pl.when(jnp.logical_not(active))
        def _():
            for name in ("o_co0", "o_co1", "o_co2", "o_co3"):
                o_copy(name, CO).wait_recv()

    def early(k, _):
        attend(k)

        @pl.when(k >= 2)
        def _():
            forward(k - 2)

        @pl.when(k == 4)
        def _():
            wait_out_weights()

        @pl.when(k >= 4)
        def _():
            foreign(k - 4)

        return 0

    lax.fori_loop(0, 8, early, 0)
    forward(6)
    forward(7)

    def late(yt, _):
        finish(yt)
        return 0

    lax.fori_loop(0, 4, late, 0)

    outs = []
    for yy in range(4):
        @pl.when(y != yy)
        def _():
            copy(ssend.at[yy], srecv.at[yy], S_Y + (y - yy + 4) % 4, YP).wait_recv()

        for zz in range(4):
            upd[yy, zz] = (latc[yy, zz].astype(F32) + srecv[yy, zz].astype(F32)).astype(BF16)
        cp = copy(upd.at[yy], out.at[yy], OUT + yy, NX)
        cp.start()
        outs.append(cp)

    for cp in sent:
        cp.wait_send()

    def drain(k, _):
        for base in (A_YP, A_YM, A_FP, A_FM):
            a_copy(k, base).wait_send()
        return 0

    lax.fori_loop(0, 8, drain, 0)

    def drain4(k, _):
        p_copy(k).wait_send()

        @pl.when(k != y)
        def _():
            s_copy(k).wait_send()

        return 0

    lax.fori_loop(0, 4, drain4, 0)

    @pl.when(jnp.logical_not(gather))
    def _():
        o_first().wait_send()

    @pl.when(gather)
    def _():
        o_copy("o_xh", XH).wait_send()

    @pl.when(active)
    def _():
        for name, dev in (("o_zp", ZP), ("o_zm", ZM), ("o_fp", ZP), ("o_fm", ZM), ("o_co0", CO), ("o_co1", CO), ("o_co2", CO), ("o_co3", CO)):
            o_copy(name, dev).wait_send()

    for cp in outs:
        cp.wait()


def body(latents, gain, mod_table, slot_noise_level, key_block_index, counts, w_qkv, w_out):
    vmem = pl.BlockSpec(memory_space=pltpu.VMEM)
    smem = pl.BlockSpec(memory_space=pltpu.SMEM)
    hbm = pl.BlockSpec(memory_space=pl.ANY)
    blocks = (4, 4, ROWS, PIECE)
    out = pl.pallas_call(
        kernel,
        out_shape=jax.ShapeDtypeStruct(blocks, BF16),
        in_specs=[vmem, vmem, vmem, smem, smem, smem, hbm, hbm],
        out_specs=hbm,
        scratch_shapes=[
            pltpu.VMEM((8, ROWS, D), BF16),
            pltpu.VMEM((D, QKV), BF16),
            pltpu.VMEM((4, 4 * GROUP, PIECE), BF16),
            pltpu.VMEM((8, ROWS, GROUP), BF16),
            pltpu.VMEM((16, ROWS, 2 * GROUP), BF16),
            pltpu.VMEM((8, ROWS, 4 * GROUP), BF16),
            pltpu.VMEM((2 * ROWS, QKV), F32),
            pltpu.VMEM(blocks, BF16),
            pltpu.VMEM(blocks, BF16),
            pltpu.VMEM(blocks, BF16),
            pltpu.VMEM(blocks, BF16),
            pltpu.VMEM(blocks, BF16),
            pltpu.VMEM(blocks, BF16),
            pltpu.SemaphoreType.DMA((4,)),
            pltpu.SemaphoreType.DMA((N_SEM,)),
            pltpu.SemaphoreType.DMA((N_SEM,)),
        ],
        compiler_params=pltpu.CompilerParams(
            collective_id=0, has_side_effects=True, vmem_limit_bytes=60 * 2**20
        ),
        name="window",
    )(latents[0], gain[None], mod_table, slot_noise_level, key_block_index[0], counts[0], w_qkv, w_out)
    return out.transpose(2, 1, 0, 3).reshape(1, ROWS, D)


def solution(mesh):
    in_specs = (
        P("slot", "tok", None),
        P(),
        P(),
        P("slot"),
        P("slot", None, None),
        P("slot", None),
        P(None, "slot", "tok"),
        P("tok", "slot"),
    )
    out_specs = P("slot", "tok", None)
    return jax.shard_map(body, mesh=mesh, in_specs=in_specs, out_specs=out_specs, check_vma=False)
```

time: 850 us -> 207 us (0.24)
  the two profiles are of different devices: /device:TPU:1 before, /device:TPU:28 now
where the time goes in v1:
time: 207 us
  Pallas kernels  200 us (97%)
  local copies, waits for them, and re-layouts  6.5 us (3%)
    pallas_call x1, Pallas kernels, body(): pl.pallas_call(kernel, out_shape=jax.ShapeDtypeStruct(blocks, BF16), in_s...  200 us

profile of v1, /device:TPU:28, one launch (start us, length us, event | category | flops | bytes accessed | tf_op | source)
XLA Modules:
  0.0 207.2 jit_solution(8332584715833545420)
XLA Ops:
  0.7 1.3 copy.11.ids
  2.0 1.8 copy.12.wo
  3.8 200.0 %window.1 = bf16[4,4,128,320]{3,2,1,0:T(8,128)(2,1)} custom-call(bf16[128,5120]{1,0:T(8,128)(2,1)} %bitcast.8, f32[1,5120]{1,0:T(1,128)} %bitcast.9, f32[16,2,5120]{2,1,0:T(2,128)} %mod.1, s32[1]{0:T(128)S(6)} %copy.15.level, s32[8,4]{1,0:T(8,128)} %copy.11.ids, s32[8]{0:T(128)} %bitcast.11, bf16[3,320,384]{2,1,0:T(8,128)(2,1)} %wq.1, bf16[384,320]{1,0:T(8,128)(2,1)} %copy.12.wo), custom_call_target="tpu_custom_call" | custom-call | tf_op jit(solution)/shard_map/window/pallas_call | solution.py:463
  203.8 1.9 copy.13
  205.7 1.4 copy.14

commit v2 on v1

v2 whole, which is shorter than its diff:
```python
import functools
import math

import jax
import jax.numpy as jnp
from jax import lax
from jax.experimental import pallas as pl
from jax.experimental.pallas import tpu as pltpu
from jax.sharding import PartitionSpec as P

MESH = pl.DeviceIdType.MESH
BF16 = jnp.bfloat16
F32 = jnp.float32

HD = 128
BLK = 128
ROWS = 128
D = 5120
QKV = 1152
PIECE = 320
HALF = 64
NTILE = 256
COLS = 1280
GROUP = 384

NAMES = (
    "w_xh", "w_zp0", "w_zm0", "w_co0", "w_zp1", "w_zm1", "w_co1", "w_fp0", "w_fm0", "w_co2", "w_co3",
    "w_fp1", "w_fm1", "w_co4", "w_co5", "w_co6", "w_co7", "t_x0", "t_x1", "t_yp0", "t_yp1", "t_ym0", "t_ym1",
    "t_fp", "t_fm", "u_yp0", "u_yp1", "u_ym0", "u_ym1", "u_fp", "u_fm", "u_x", "o_a0", "o_a1", "o_a2",
    "o_a3", "o_xh", "o_zp", "o_zm", "o_fp", "o_fm", "o_co0", "o_co1", "o_co2", "o_co3",
)
SEM = {name: i for i, name in enumerate(NAMES)}
KV0 = len(NAMES)
A_YP = KV0 + 8
A_YM = A_YP + 8
A_FP = A_YM + 8
A_FM = A_FP + 8
P_X = A_FM + 8
S_Y = P_X + 4
LAT = S_Y + 4
N_SEM = LAT + 1
ORDER = (3, 1, 2, 0)
SEND_P = (1, 2, 3, 0)
SEND_M = (3, 2, 0, 1)
FORWARD = (2, 3, 0, 1)


def kernel(lat, gain, mod, level, ids, counts, wq, wo, branch, lat_prev,
           x, w, wot, wout, q, ctx, att, psend, precv, ssend, local, ss, rs):
    s, t = lax.axis_index("slot"), lax.axis_index("tok")
    z, h, c = s // 4, (s // 2) % 2, s % 2
    y, l = t // 2, t % 2

    def slot(zz, hh, cc):
        return (zz % 4) * 4 + hh * 2 + cc

    def tok(yy, ll):
        return (yy % 4) * 2 + ll

    XL = (s, tok(y, 1 - l))
    YP, YM, Y2 = (s, tok(y + 1, l)), (s, tok(y + 3, l)), (s, tok(y + 2, l))
    ZP, ZM = (slot(z + 1, h, c), t), (slot(z + 3, h, c), t)
    XH, CO = (slot(z, 1 - h, c), t), (slot(z, h, 1 - c), t)
    NX, PV = ((s + 1) % 16, t), ((s + 15) % 16, t)

    def copy(src, dst, sem, dev):
        k = SEM[sem] if isinstance(sem, str) else sem
        return pltpu.make_async_remote_copy(
            src_ref=src, dst_ref=dst, send_sem=ss.at[k], recv_sem=rs.at[k], device_id=dev, device_id_type=MESH
        )

    sent = []

    def send(ref, sem, dev):
        cp = copy(ref, ref, sem, dev)
        cp.start()
        sent.append(cp)
        return cp

    barrier = pltpu.get_barrier_semaphore()
    here, before = (l + c) % 2, (l + 1 - c) % 2
    peers = [XL, YP, YM, Y2, ZP, ZM, XH, CO, NX, PV]
    peers += [(NX[0], tok(yy, here)) for yy in range(4)] + [(PV[0], tok(yy, before)) for yy in range(4)]
    for dev in peers:
        pl.semaphore_signal(barrier, inc=1, device_id=dev, device_id_type=MESH)

    def wrows(piece, first=0, size=PIECE):
        return w.at[pl.ds(pl.multiple_of(piece * PIECE + first, 32), size)]

    own = [
        pltpu.make_async_copy(
            wq.at[j], w.at[pl.ds(pl.multiple_of(s * PIECE, 64), PIECE), pl.ds(j * GROUP, GROUP)], local.at[j]
        )
        for j in range(3)
    ]
    for cp in own:
        cp.start()
    for cp in own:
        cp.wait()
    pl.semaphore_wait(barrier, len(peers))

    mine = wrows(s)
    w_xh = send(mine, "w_xh", XH)
    w_zp0 = send(mine, "w_zp0", ZP)
    w_zm0 = send(mine, "w_zm0", ZM)
    w_co = [send(mine, "w_co0", CO)]

    lv = level[0]
    factor = gain[...] * (1.0 + mod[lv, 0:1, :])
    offset = mod[lv, 1:2, :]

    def norm(i, _):
        rows = pl.ds(pl.multiple_of(i * 16, 16), 16)
        xf = lat[rows, :].astype(F32)
        mean = jnp.mean(xf, axis=-1, keepdims=True)
        centred = xf - mean
        var = jnp.mean(centred * centred, axis=-1, keepdims=True)
        x[t, rows, :] = (centred * lax.rsqrt(var + 1e-06) * factor + offset).astype(BF16)
        return 0

    def shard(tt, half):
        return x.at[tt, pl.ds(half * HALF, HALF)]

    t_x, t_yp, t_ym = [], [], []
    for half in range(2):
        lax.fori_loop(half * 4, half * 4 + 4, norm, 0)
        t_yp.append(send(shard(t, half), "t_yp%d" % half, YP))
        t_ym.append(send(shard(t, half), "t_ym%d" % half, YM))
        t_x.append(send(shard(t, half), "t_x%d" % half, XL))

    yd = 2 * h + c
    gather = y == yd
    active = c == y % 2
    relay = active & (h != y // 2)

    def ocols(zz):
        return pl.ds(pl.multiple_of((zz % 4) * PIECE, 64), PIECE)

    def lanes(yy):
        return pl.ds(pl.multiple_of((yy % 4) * GROUP, 128), GROUP)

    def o_first():
        return copy(wo, wot.at[ocols(z), lanes(y)], SEM["o_a0"] + (y - yd + 4) % 4, (s, tok(yd, l)))

    def o_copy(name, dev, zz):
        ref = wot.at[ocols(zz)]
        if name == "o_fp":
            ref = wot.at[ocols(zz), pl.ds(0, 768)]
        elif name == "o_fm":
            ref = wot.at[ocols(zz), pl.ds(768, 768)]
        return copy(ref, ref, name, dev)

    @pl.when(jnp.logical_not(gather))
    def _():
        o_first().start()

    @pl.when(gather)
    def _():
        cp = pltpu.make_async_copy(wo, wot.at[ocols(z), lanes(y)], local.at[3])
        cp.start()
        cp.wait()

    tm, tp, tx = tok(y + 3, l), tok(y + 1, l), tok(y, 1 - l)
    t2 = tok(y + 2, l)
    um, up, u2 = tok(y + 3, 1 - l), tok(y + 1, 1 - l), tok(y + 2, 1 - l)

    @pl.when(gather)
    def _():
        for d in range(1, 4):
            src = wot.at[ocols(z), lanes(0)]
            copy(src, src, SEM["o_a0"] + d, YP).wait_recv()
        o_copy("o_xh", XH, z).start()

    t_yp[0].wait_recv()
    t_fp = send(shard(tm, 0), "t_fp", YP)
    w_zp0.wait_recv()
    pm = slot(z + 3, h, c)
    w_fp0 = send(wrows(pm, 0, PIECE // 2), "w_fp0", ZP)
    w_co.append(send(wrows(pm), "w_co2", CO))
    w_zm0.wait_recv()
    pp = slot(z + 1, h, c)
    w_fm0 = send(wrows(pp, PIECE // 2, PIECE // 2), "w_fm0", ZM)
    w_co.append(send(wrows(pp), "w_co3", CO))
    w_xh.wait_recv()
    px = slot(z, 1 - h, c)
    w_zp1 = send(wrows(px), "w_zp1", ZP)
    w_zm1 = send(wrows(px), "w_zm1", ZM)
    w_co.append(send(wrows(px), "w_co1", CO))
    u_yp, u_ym = [], []

    def second(half):
        t_x[half].wait_recv()
        u_yp.append(send(shard(tx, half), "u_yp%d" % half, YP))
        u_ym.append(send(shard(tx, half), "u_ym%d" % half, YM))

    second(0)
    t_ym[1].wait_recv()
    t_fm = send(shard(tp, 1), "t_fm", YM)
    second(1)

    w_zp1.wait_recv()
    pm1 = slot(z + 3, 1 - h, c)
    w_fp1 = send(wrows(pm1, 0, PIECE // 2), "w_fp1", ZP)
    w_co.append(send(wrows(pm1), "w_co4", CO))
    w_zm1.wait_recv()
    pp1 = slot(z + 1, 1 - h, c)
    w_fm1 = send(wrows(pp1, PIECE // 2, PIECE // 2), "w_fm1", ZM)
    w_co.append(send(wrows(pp1), "w_co5", CO))

    @pl.when(relay)
    def _():
        o_copy("o_xh", XH, z).wait_recv()

    @pl.when(active)
    def _():
        o_copy("o_zp", ZP, z).start()
        o_copy("o_zm", ZM, z).start()
        o_copy("o_co0", CO, z).start()

    w_fp0.wait_recv()
    w_fm0.wait_recv()
    w_co.append(send(wrows(slot(z + 2, h, c)), "w_co6", CO))
    t_fm.wait_recv()
    u_x = send(shard(t2, 1), "u_x", XL)

    w_fp1.wait_recv()
    w_fm1.wait_recv()
    w_co.append(send(wrows(slot(z + 2, 1 - h, c)), "w_co7", CO))
    for cp in w_co:
        cp.wait_recv()

    def quarter(tt, part):
        return x.at[tt, pl.ds(part * 32, 32)]

    def u_forward():
        a, b = quarter(um, 0), quarter(up, 1)
        return copy(a, a, "u_fp", YP), copy(b, b, "u_fm", YM)

    def kv_copy(tt, k):
        return copy(ctx.at[tt], ctx.at[8 + tt], KV0 + k, NX)

    def project(b, _):
        @pl.when(b == 1)
        def _():
            t_yp[1].wait_recv()
            t_ym[0].wait_recv()

        @pl.when(b == 2)
        def _():
            u_yp[1].wait_recv()
            u_ym[1].wait_recv()

        @pl.when(b == 3)
        def _():
            t_fp.wait_recv()
            u_x.wait_recv()
            for cp in u_forward():
                cp.wait_recv()

        def pick(values):
            return jnp.where(b == 0, values[0], jnp.where(b == 1, values[1], jnp.where(b == 2, values[2], values[3])))

        ta, tb = pick((t, tm, um, t2)), pick((tx, tp, up, u2))
        rows = jnp.concatenate([x[ta], x[tb]], axis=0)
        for n in range(3):
            cols = slice(n * NTILE, (n + 1) * NTILE)
            part = jnp.dot(rows, w[:, GROUP + n * NTILE:GROUP + (n + 1) * NTILE], preferred_element_type=F32).astype(BF16)
            ctx[ta, :, cols] = part[:ROWS]
            ctx[tb, :, cols] = part[ROWS:]
        kv_copy(ta, 2 * b).start()
        kv_copy(tb, 2 * b + 1).start()
        part = jnp.dot(rows, w[:, :GROUP], preferred_element_type=F32).astype(BF16)
        q[ta] = part[:ROWS]
        q[tb] = part[ROWS:]
        return 0

    u_yp[0].wait_recv()
    u_ym[0].wait_recv()
    for cp in u_forward():
        cp.start()
    lax.fori_loop(0, 4, project, 0)
    lat_copy = copy(lat, lat_prev, LAT, NX)
    lat_copy.start()

    @pl.when(active)
    def _():
        o_copy("o_zp", ZP, z + 3).wait_recv()
        o_copy("o_fp", ZP, z + 3).start()
        o_copy("o_co1", CO, z + 3).start()
        o_copy("o_zm", ZM, z + 1).wait_recv()
        o_copy("o_fm", ZM, z + 1).start()
        o_copy("o_co2", CO, z + 1).start()

    for k in range(8):
        kv_copy(t, k).wait_recv()

    scale = 1.0 / math.sqrt(HD)

    def owner(j):
        return (y + 1 + j) % 4

    def tile_at(yt, second_half):
        return 2 * (yt % 4) + jnp.where(second_half, here, 1 - here)

    def a_copy(j, late, base):
        if base == A_YP:
            ref, dev = att.at[tile_at(y + 1 + j, late), :, lanes(y)], YP
        elif base == A_YM:
            ref, dev = att.at[tile_at(y + 1 + j, late), :, lanes(y)], YM
        elif base == A_FP:
            ref, dev = att.at[tile_at(y + j, late), pl.ds(0, HALF), lanes(y + 3)], YP
        else:
            ref, dev = att.at[tile_at(y + 2 + j, late), pl.ds(HALF, HALF), lanes(y + 1)], YM
        return copy(ref, ref, base + j + jnp.where(late, 4, 0), dev)

    def at(k, values):
        return jnp.where(k == 0, values[0], jnp.where(k == 1, values[1], jnp.where(k == 2, values[2], values[3])))

    def attend(i):
        listed = [ids[j, i] for j in range(4)]
        valid = []
        for j in range(4):
            ok = j < counts[i]
            for e in range(j):
                ok = ok & (listed[e] != listed[j])
            valid.append(ok)
        outs = []
        for head in range(3):
            hc = slice(head * HD, (head + 1) * HD)
            vc = slice(GROUP + head * HD, GROUP + (head + 1) * HD)
            keys = jnp.concatenate([ctx[listed[j], :, hc] for j in range(4)], axis=0)
            scores = lax.dot_general(q[i, :, hc], keys, (((1,), (1,)), ((), ())), preferred_element_type=F32) * scale
            scores = [jnp.where(valid[j], scores[:, j * BLK:(j + 1) * BLK], -1e30) for j in range(4)]
            top = jnp.maximum(jnp.maximum(scores[0], scores[1]), jnp.maximum(scores[2], scores[3]))
            top = jnp.max(top, axis=1, keepdims=True)
            expo = [jnp.exp(sc - top) for sc in scores]
            total = jnp.sum((expo[0] + expo[1]) + (expo[2] + expo[3]), axis=1, keepdims=True)
            probs = jnp.concatenate([(e / total).astype(BF16) for e in expo], axis=1)
            values = jnp.concatenate([ctx[listed[j], :, vc] for j in range(4)], axis=0)
            outs.append(jnp.dot(probs, values, preferred_element_type=F32).astype(BF16))
        att[i, :, lanes(y)] = jnp.concatenate(outs, axis=1)

    def forward(k, late):
        j = at(k, FORWARD)
        a_copy(j, late, A_YP).wait_recv()
        a_copy(j, late, A_FP).start()
        a_copy(j, late, A_YM).wait_recv()
        a_copy(j, late, A_FM).start()

    def attention(k, _):
        late = k >= 4
        j = at(k % 4, ORDER)
        attend(tile_at(y + 1 + j, late))

        @pl.when(k == 0)
        def _():
            a_copy(3, False, A_YM).start()

        @pl.when(k == 1)
        def _():
            a_copy(1, False, A_YP).start()

        @pl.when(k == 2)
        def _():
            a_copy(2, False, A_YP).start()
            a_copy(2, False, A_YM).start()

        @pl.when(k == 3)
        def _():
            a_copy(0, False, A_YM).start()
            a_copy(3, False, A_YP).start()
            a_copy(1, False, A_YM).start()
            a_copy(0, False, A_YP).start()

        @pl.when(late)
        def _():
            a_copy(j, True, A_YP).start()
            a_copy(j, True, A_YM).start()
            forward(k - 4, False)

        return 0

    lax.fori_loop(0, 8, attention, 0)

    CORE = ("o_co0", "o_co1", "o_co2", "o_co3")

    @pl.when(active)
    def _():
        o_copy("o_fp", ZP, z + 2).wait_recv()
        o_copy("o_fm", ZM, z + 2).wait_recv()
        o_copy("o_co3", CO, z + 2).start()

    @pl.when(jnp.logical_not(active))
    def _():
        for name in CORE:
            o_copy(name, CO, z).wait_recv()

    def turn(r, _):
        rows = pl.ds(pl.multiple_of(r * 128, 128), 128)
        wout[:, rows] = wot[rows, :].T
        return 0

    lax.fori_loop(0, 10, turn, 0)

    def product(p, late):
        j = (p + 2) % 4
        a_copy(j, late, A_FP).wait_recv()
        a_copy(j, late, A_FM).wait_recv()
        return jnp.dot(att[tile_at(y + 1 + p, late)], wout[...], preferred_element_type=F32)

    def p_copy(p):
        return copy(psend.at[p], precv.at[p], P_X + p, XL)

    def foreign(p, _):
        psend[p] = product(p, False).astype(BF16)
        p_copy(p).start()
        forward(p, True)
        return 0

    lax.fori_loop(0, 4, foreign, 0)

    def s_copy(p):
        return copy(ssend.at[p], branch.at[y], S_Y + p, (NX[0], tok(y + 1 + p, here)))

    def finish(p, _):
        mine = product(p, True)
        p_copy(p).wait_recv()
        ssend[p] = (mine + precv[p].astype(F32)).astype(BF16)
        s_copy(p).start()
        return 0

    lax.fori_loop(0, 4, finish, 0)

    for cp in sent:
        cp.wait_send()
    for cp in u_forward():
        cp.wait_send()

    def drain(k, _):
        kv_copy(t, k).wait_send()
        for base in (A_YP, A_YM, A_FP, A_FM):
            a_copy(k % 4, k >= 4, base).wait_send()
        return 0

    lax.fori_loop(0, 8, drain, 0)
    for p in range(4):
        p_copy(p).wait_send()
        s_copy(p).wait_send()
    lat_copy.wait_send()

    @pl.when(jnp.logical_not(gather))
    def _():
        o_first().wait_send()

    @pl.when(gather)
    def _():
        o_copy("o_xh", XH, z).wait_send()

    @pl.when(active)
    def _():
        for name in ("o_zp", "o_zm", "o_fp", "o_fm") + CORE:
            o_copy(name, CO, z).wait_send()

    lat_copy.wait_recv()
    for p in range(4):
        s_copy(p).wait_recv()


def residual(branch, lat, out):
    for zz in range(4):
        cols = slice(zz * COLS, (zz + 1) * COLS)
        pieces = [branch[yy, :, zz * PIECE:(zz + 1) * PIECE].astype(F32) for yy in range(4)]
        out[:, cols] = (lat[:, cols].astype(F32) + jnp.concatenate(pieces, axis=1)).astype(BF16)


def body(latents, gain, mod_table, slot_noise_level, key_block_index, counts, w_qkv, w_out):
    vmem = pl.BlockSpec(memory_space=pltpu.VMEM)
    smem = pl.BlockSpec(memory_space=pltpu.SMEM)
    hbm = pl.BlockSpec(memory_space=pl.ANY)
    blocks = pltpu.VMEM((4, ROWS, COLS), BF16)
    branch, lat_prev = pl.pallas_call(
        kernel,
        out_shape=[jax.ShapeDtypeStruct((4, ROWS, COLS), BF16), jax.ShapeDtypeStruct((ROWS, D), BF16)],
        in_specs=[vmem, vmem, vmem, smem, smem, smem, hbm, hbm],
        out_specs=[hbm, hbm],
        scratch_shapes=[
            pltpu.VMEM((8, ROWS, D), BF16),
            pltpu.VMEM((D, QKV), BF16),
            pltpu.VMEM((COLS, 4 * GROUP), BF16),
            pltpu.VMEM((4 * GROUP, COLS), BF16),
            pltpu.VMEM((8, ROWS, GROUP), BF16),
            pltpu.VMEM((16, ROWS, 2 * GROUP), BF16),
            pltpu.VMEM((8, ROWS, 4 * GROUP), BF16),
            blocks,
            blocks,
            blocks,
            pltpu.SemaphoreType.DMA((4,)),
            pltpu.SemaphoreType.DMA((N_SEM,)),
            pltpu.SemaphoreType.DMA((N_SEM,)),
        ],
        compiler_params=pltpu.CompilerParams(
            collective_id=0, has_side_effects=True, vmem_limit_bytes=60 * 2**20
        ),
        name="window",
    )(latents[0], gain[None], mod_table, slot_noise_level, key_block_index[0].T, counts[0], w_qkv, w_out.T)
    out = pl.pallas_call(
        residual,
        grid=(4,),
        out_shape=jax.ShapeDtypeStruct((ROWS, D), BF16),
        in_specs=[pl.BlockSpec((4, ROWS // 4, COLS), lambda i: (0, i, 0)), pl.BlockSpec((ROWS // 4, D), lambda i: (i, 0))],
        out_specs=pl.BlockSpec((ROWS // 4, D), lambda i: (i, 0)),
        name="residual",
    )(branch, lat_prev)
    return out[None]


def solution(mesh):
    in_specs = (
        P("slot", "tok", None),
        P(),
        P(),
        P("slot"),
        P("slot", None, None),
        P("slot", None),
        P(None, "slot", "tok"),
        P("tok", "slot"),
    )
    out_specs = P("slot", "tok", None)
    return jax.shard_map(body, mesh=mesh, in_specs=in_specs, out_specs=out_specs, check_vma=False)
```

time: 207 us -> 168 us (0.81)
  the two profiles are of different devices: /device:TPU:28 before, /device:TPU:1 now
where the time goes in v2:
time: 168 us
  Pallas kernels  167 us (99%)
    pallas_call x1, Pallas kernels, body(): pl.pallas_call(kernel, out_shape=[jax.ShapeDtypeStruct((4, ROWS, COLS), B...  163 us
    pallas_call x1, Pallas kernels, body(): pl.pallas_call(residual, grid=(4,), out_shape=jax.ShapeDtypeStruct((ROWS,...  3.93 us

profile of v2, /device:TPU:1, one launch (start us, length us, event | category | flops | bytes accessed | tf_op | source)
XLA Modules:
  0.0 167.9 jit_solution(15179061417777959487)
XLA Ops:
  0.7 163.3 %window.1 = (bf16[4,128,1280]{2,1,0:T(8,128)(2,1)}, bf16[128,5120]{1,0:T(8,128)(2,1)}) custom-call(bf16[128,5120]{1,0:T(8,128)(2,1)} %bitcast.8, f32[1,5120]{1,0:T(1,128)} %bitcast.10, f32[16,2,5120]{2,1,0:T(2,128)} %mod.1, s32[1]{0:T(128)S(6)} %copy.9.level, s32[4,8]{1,0:T(4,128)} %bitcast.11, s32[8]{0:T(128)} %bitcast.12, bf16[3,320,384]{2,1,0:T(8,128)(2,1)} %wq.1, ...), custom_call_target="tpu_custom_call" | custom-call | tf_op jit(solution)/shard_map/window/pallas_call | solution.py:481
  164.0 3.9 %residual.1 = bf16[128,5120]{1,0:T(8,128)(2,1)} custom-call(bf16[4,128,1280]{2,1,0:T(8,128)(2,1)} %get-tuple-element.7.branch, bf16[128,5120]{1,0:T(8,128)(2,1)} %get-tuple-element.8.lat), custom_call_target="tpu_custom_call" | custom-call | tf_op jit(solution)/shard_map/residual/pallas_call | solution.py:506

commit v3 on v2

--- a/solution.py
+++ b/solution.py
@@ -27,11 +27,11 @@
     "w_xh", "w_zp0", "w_zm0", "w_co0", "w_zp1", "w_zm1", "w_co1", "w_fp0", "w_fm0", "w_co2", "w_co3",
     "w_fp1", "w_fm1", "w_co4", "w_co5", "w_co6", "w_co7", "t_x0", "t_x1", "t_yp0", "t_yp1", "t_ym0", "t_ym1",
     "t_fp", "t_fm", "u_yp0", "u_yp1", "u_ym0", "u_ym1", "u_fp", "u_fm", "u_x", "o_a0", "o_a1", "o_a2",
-    "o_a3", "o_xh", "o_zp", "o_zm", "o_fp", "o_fm", "o_co0", "o_co1", "o_co2", "o_co3",
+    "o_a3", "o_xh", "o_zp", "o_zm", "o_z2", "o_co0", "o_co1", "o_co2", "o_co3",
 )
 SEM = {name: i for i, name in enumerate(NAMES)}
 KV0 = len(NAMES)
-A_YP = KV0 + 8
+A_YP = KV0 + 16
 A_YM = A_YP + 8
 A_FP = A_YM + 8
 A_FM = A_FP + 8
@@ -95,16 +95,6 @@
     ]
     for cp in own:
         cp.start()
-    for cp in own:
-        cp.wait()
-    pl.semaphore_wait(barrier, len(peers))
-
-    mine = wrows(s)
-    w_xh = send(mine, "w_xh", XH)
-    w_zp0 = send(mine, "w_zp0", ZP)
-    w_zm0 = send(mine, "w_zm0", ZM)
-    w_co = [send(mine, "w_co0", CO)]
-
     lv = level[0]
     factor = gain[...] * (1.0 + mod[lv, 0:1, :])
     offset = mod[lv, 1:2, :]
@@ -118,15 +108,10 @@
         x[t, rows, :] = (centred * lax.rsqrt(var + 1e-06) * factor + offset).astype(BF16)
         return 0
 
-    def shard(tt, half):
-        return x.at[tt, pl.ds(half * HALF, HALF)]
-
-    t_x, t_yp, t_ym = [], [], []
-    for half in range(2):
-        lax.fori_loop(half * 4, half * 4 + 4, norm, 0)
-        t_yp.append(send(shard(t, half), "t_yp%d" % half, YP))
-        t_ym.append(send(shard(t, half), "t_ym%d" % half, YM))
-        t_x.append(send(shard(t, half), "t_x%d" % half, XL))
+    lax.fori_loop(0, 4, norm, 0)
+    for cp in own:
+        cp.wait()
+    pl.semaphore_wait(barrier, len(peers))
 
     yd = 2 * h + c
     gather = y == yd
@@ -144,10 +129,6 @@
 
     def o_copy(name, dev, zz):
         ref = wot.at[ocols(zz)]
-        if name == "o_fp":
-            ref = wot.at[ocols(zz), pl.ds(0, 768)]
-        elif name == "o_fm":
-            ref = wot.at[ocols(zz), pl.ds(768, 768)]
         return copy(ref, ref, name, dev)
 
     @pl.when(jnp.logical_not(gather))
@@ -159,6 +140,23 @@
         cp = pltpu.make_async_copy(wo, wot.at[ocols(z), lanes(y)], local.at[3])
         cp.start()
         cp.wait()
+
+    mine = wrows(s)
+    w_xh = send(mine, "w_xh", XH)
+    w_zp0 = send(mine, "w_zp0", ZP)
+    w_zm0 = send(mine, "w_zm0", ZM)
+    w_co = [send(mine, "w_co0", CO)]
+
+    def shard(tt, half):
+        return x.at[tt, pl.ds(half * HALF, HALF)]
+
+    t_x, t_yp, t_ym = [], [], []
+    for half in range(2):
+        if half == 1:
+            lax.fori_loop(4, 8, norm, 0)
+        t_yp.append(send(shard(t, half), "t_yp%d" % half, YP))
+        t_ym.append(send(shard(t, half), "t_ym%d" % half, YM))
+        t_x.append(send(shard(t, half), "t_x%d" % half, XL))
 
     tm, tp, tx = tok(y + 3, l), tok(y + 1, l), tok(y, 1 - l)
     t2 = tok(y + 2, l)
@@ -207,15 +205,17 @@
     w_fm1 = send(wrows(pp1, PIECE // 2, PIECE // 2), "w_fm1", ZM)
     w_co.append(send(wrows(pp1), "w_co5", CO))
 
+    def spread():
+        for name, dev in (("o_zp", ZP), ("o_zm", ZM), ("o_co0", CO)):
+            o_copy(name, dev, z).start()
+
     @pl.when(relay)
     def _():
         o_copy("o_xh", XH, z).wait_recv()
 
     @pl.when(active)
     def _():
-        o_copy("o_zp", ZP, z).start()
-        o_copy("o_zm", ZM, z).start()
-        o_copy("o_co0", CO, z).start()
+        spread()
 
     w_fp0.wait_recv()
     w_fm0.wait_recv()
@@ -236,23 +236,29 @@
         a, b = quarter(um, 0), quarter(up, 1)
         return copy(a, a, "u_fp", YP), copy(b, b, "u_fm", YM)
 
-    def kv_copy(tt, k):
-        return copy(ctx.at[tt], ctx.at[8 + tt], KV0 + k, NX)
+    def kv_copy(tt, half, k):
+        rows = pl.ds(pl.multiple_of(half * HALF, HALF), HALF)
+        return copy(ctx.at[tt, rows], ctx.at[8 + tt, rows], KV0 + k, NX)
 
     def project(b, _):
         @pl.when(b == 1)
         def _():
+            @pl.when(active)
+            def _():
+                o_copy("o_zm", ZM, z + 1).wait_recv()
+                o_copy("o_z2", ZM, z + 1).start()
+
             t_yp[1].wait_recv()
             t_ym[0].wait_recv()
 
         @pl.when(b == 2)
         def _():
+            t_fp.wait_recv()
+
+        @pl.when(b == 3)
+        def _():
             u_yp[1].wait_recv()
             u_ym[1].wait_recv()
-
-        @pl.when(b == 3)
-        def _():
-            t_fp.wait_recv()
             u_x.wait_recv()
             for cp in u_forward():
                 cp.wait_recv()
@@ -260,18 +266,25 @@
         def pick(values):
             return jnp.where(b == 0, values[0], jnp.where(b == 1, values[1], jnp.where(b == 2, values[2], values[3])))
 
-        ta, tb = pick((t, tm, um, t2)), pick((tx, tp, up, u2))
-        rows = jnp.concatenate([x[ta], x[tb]], axis=0)
+        first = pick((0, 0, 0, 1))
+        parts = (
+            (pick((t, tm, um, um)), first),
+            (pick((t, tm, up, up)), pick((1, 1, 0, 1))),
+            (pick((tx, tp, t2, u2)), 0),
+            (pick((tx, tp, t2, u2)), 1),
+        )
+        parts = [(tt, half, pl.ds(pl.multiple_of(half * HALF, HALF), HALF)) for tt, half in parts]
+        rows = jnp.concatenate([x[tt, rr, :] for tt, half, rr in parts], axis=0)
         for n in range(3):
             cols = slice(n * NTILE, (n + 1) * NTILE)
             part = jnp.dot(rows, w[:, GROUP + n * NTILE:GROUP + (n + 1) * NTILE], preferred_element_type=F32).astype(BF16)
-            ctx[ta, :, cols] = part[:ROWS]
-            ctx[tb, :, cols] = part[ROWS:]
-        kv_copy(ta, 2 * b).start()
-        kv_copy(tb, 2 * b + 1).start()
+            for i, (tt, half, rr) in enumerate(parts):
+                ctx[tt, rr, cols] = part[i * HALF:(i + 1) * HALF]
+        for i, (tt, half, rr) in enumerate(parts):
+            kv_copy(tt, half, 4 * b + i).start()
         part = jnp.dot(rows, w[:, :GROUP], preferred_element_type=F32).astype(BF16)
-        q[ta] = part[:ROWS]
-        q[tb] = part[ROWS:]
+        for i, (tt, half, rr) in enumerate(parts):
+            q[tt, rr, :] = part[i * HALF:(i + 1) * HALF]
         return 0
 
     u_yp[0].wait_recv()
@@ -279,20 +292,19 @@
     for cp in u_forward():
         cp.start()
     lax.fori_loop(0, 4, project, 0)
+
     lat_copy = copy(lat, lat_prev, LAT, NX)
     lat_copy.start()
 
+    for k in range(16):
+        kv_copy(t, 0, k).wait_recv()
+
     @pl.when(active)
     def _():
-        o_copy("o_zp", ZP, z + 3).wait_recv()
-        o_copy("o_fp", ZP, z + 3).start()
-        o_copy("o_co1", CO, z + 3).start()
-        o_copy("o_zm", ZM, z + 1).wait_recv()
-        o_copy("o_fm", ZM, z + 1).start()
-        o_copy("o_co2", CO, z + 1).start()
-
-    for k in range(8):
-        kv_copy(t, k).wait_recv()
+        for name, dz, onward in (("o_zp", 3, "o_co1"), ("o_zm", 1, "o_co2"), ("o_z2", 2, "o_co3")):
+            if name != "o_zm":
+                o_copy(name, ZP, z + dz).wait_recv()
+            o_copy(onward, CO, z + dz).start()
 
     scale = 1.0 / math.sqrt(HD)
 
@@ -384,12 +396,6 @@
 
     CORE = ("o_co0", "o_co1", "o_co2", "o_co3")
 
-    @pl.when(active)
-    def _():
-        o_copy("o_fp", ZP, z + 2).wait_recv()
-        o_copy("o_fm", ZM, z + 2).wait_recv()
-        o_copy("o_co3", CO, z + 2).start()
-
     @pl.when(jnp.logical_not(active))
     def _():
         for name in CORE:
@@ -437,7 +443,8 @@
         cp.wait_send()
 
     def drain(k, _):
-        kv_copy(t, k).wait_send()
+        kv_copy(t, 0, 2 * k).wait_send()
+        kv_copy(t, 0, 2 * k + 1).wait_send()
         for base in (A_YP, A_YM, A_FP, A_FM):
             a_copy(k % 4, k >= 4, base).wait_send()
         return 0
@@ -458,7 +465,7 @@
 
     @pl.when(active)
     def _():
-        for name in ("o_zp", "o_zm", "o_fp", "o_fm") + CORE:
+        for name in ("o_zp", "o_zm", "o_z2") + CORE:
             o_copy(name, CO, z).wait_send()
 
     lat_copy.wait_recv()
@@ -469,8 +476,8 @@
 def residual(branch, lat, out):
     for zz in range(4):
         cols = slice(zz * COLS, (zz + 1) * COLS)
-        pieces = [branch[yy, :, zz * PIECE:(zz + 1) * PIECE].astype(F32) for yy in range(4)]
-        out[:, cols] = (lat[:, cols].astype(F32) + jnp.concatenate(pieces, axis=1)).astype(BF16)
+        pieces = [branch[yy, :, zz * PIECE:(zz + 1) * PIECE] for yy in range(4)]
+        out[:, cols] = (lat[:, cols].astype(F32) + jnp.concatenate(pieces, axis=1).astype(F32)).astype(BF16)
 
 
 def body(latents, gain, mod_table, slot_noise_level, key_block_index, counts, w_qkv, w_out):
@@ -505,10 +512,10 @@
     )(latents[0], gain[None], mod_table, slot_noise_level, key_block_index[0].T, counts[0], w_qkv, w_out.T)
     out = pl.pallas_call(
         residual,
-        grid=(4,),
+        grid=(2,),
         out_shape=jax.ShapeDtypeStruct((ROWS, D), BF16),
-        in_specs=[pl.BlockSpec((4, ROWS // 4, COLS), lambda i: (0, i, 0)), pl.BlockSpec((ROWS // 4, D), lambda i: (i, 0))],
-        out_specs=pl.BlockSpec((ROWS // 4, D), lambda i: (i, 0)),
+        in_specs=[pl.BlockSpec((4, ROWS // 2, COLS), lambda i: (0, i, 0)), pl.BlockSpec((ROWS // 2, D), lambda i: (i, 0))],
+        out_specs=pl.BlockSpec((ROWS // 2, D), lambda i: (i, 0)),
         name="residual",
     )(branch, lat_prev)
     return out[None]

time: 168 us -> 157 us (0.935); the launches traced: 168 us -> 155 us
  Pallas kernels: 167 us -> 154 us
    pallas_call x1, Pallas kernels: 163 us -> 152 us  [body(): pl.pallas_call(kernel, out_shape=[jax.ShapeDtypeStruct((4, ROWS, COLS), B...]
where the time goes in v3:
time: 157 us; the launch traced here: 155 us
  Pallas kernels  154 us (98%)
    pallas_call x1, Pallas kernels, body(): pl.pallas_call(kernel, out_shape=[jax.ShapeDtypeStruct((4, ROWS, COLS), B...  152 us

profile of v3, /device:TPU:1, one launch (start us, length us, event | category | flops | bytes accessed | tf_op | source)
XLA Modules:
  0.0 155.1 jit_solution(5034497444526465729)
XLA Ops:
  0.7 151.7 %window.1 = (bf16[4,128,1280]{2,1,0:T(8,128)(2,1)}, bf16[128,5120]{1,0:T(8,128)(2,1)}) custom-call(bf16[128,5120]{1,0:T(8,128)(2,1)} %bitcast.8, f32[1,5120]{1,0:T(1,128)} %bitcast.10, f32[16,2,5120]{2,1,0:T(2,128)} %mod.1, s32[1]{0:T(128)S(6)} %copy.9.level, s32[4,8]{1,0:T(4,128)} %bitcast.11, s32[8]{0:T(128)} %bitcast.12, bf16[3,320,384]{2,1,0:T(8,128)(2,1)} %wq.1, ...), custom_call_target="tpu_custom_call" | custom-call | tf_op jit(solution)/shard_map/window/pallas_call | solution.py:488
  152.4 2.8 %residual.1 = bf16[128,5120]{1,0:T(8,128)(2,1)} custom-call(bf16[4,128,1280]{2,1,0:T(8,128)(2,1)} %get-tuple-element.7.branch, bf16[128,5120]{1,0:T(8,128)(2,1)} %get-tuple-element.8.lat), custom_call_target="tpu_custom_call" | custom-call | tf_op jit(solution)/shard_map/residual/pallas_call | solution.py:513

commit v4 on v3

--- a/solution.py
+++ b/solution.py
@@ -38,15 +38,13 @@
 P_X = A_FM + 8
 S_Y = P_X + 4
 LAT = S_Y + 4
-N_SEM = LAT + 1
-ORDER = (3, 1, 2, 0)
-SEND_P = (1, 2, 3, 0)
-SEND_M = (3, 2, 0, 1)
-FORWARD = (2, 3, 0, 1)
+LAT_Y = LAT + 1
+N_SEM = LAT_Y + 4
+ORDER = (2, 1, 3, 0)
 
 
 def kernel(lat, gain, mod, level, ids, counts, wq, wo, branch, lat_prev,
-           x, w, wot, wout, q, ctx, att, psend, precv, ssend, local, ss, rs):
+           x, w, wot, wout, q, ctx, att, psend, precv, ssend, latc, latr, local, ss, rs):
     s, t = lax.axis_index("slot"), lax.axis_index("tok")
     z, h, c = s // 4, (s // 2) % 2, s % 2
     y, l = t // 2, t % 2
@@ -157,6 +155,22 @@
         t_yp.append(send(shard(t, half), "t_yp%d" % half, YP))
         t_ym.append(send(shard(t, half), "t_ym%d" % half, YM))
         t_x.append(send(shard(t, half), "t_x%d" % half, XL))
+
+    @pl.when(c == 0)
+    def _():
+        copy(lat, lat_prev, LAT, NX).start()
+
+    def lat_copy(d):
+        return copy(latc.at[(y + d) % 4], latr.at[y], LAT_Y + d, (s, tok(y + d, l)))
+
+    def spread_latents():
+        for yy in range(4):
+            for zz in range(4):
+                first = zz * COLS + yy * PIECE
+                latc[yy, :, zz * PIECE:(zz + 1) * PIECE] = lat[:, first:first + PIECE]
+        latr[y] = latc[y]
+
+    pl.when(c == 1)(spread_latents)
 
     tm, tp, tx = tok(y + 3, l), tok(y + 1, l), tok(y, 1 - l)
     t2 = tok(y + 2, l)
@@ -255,24 +269,19 @@
         def _():
             t_fp.wait_recv()
 
-        @pl.when(b == 3)
-        def _():
-            u_yp[1].wait_recv()
-            u_ym[1].wait_recv()
-            u_x.wait_recv()
-            for cp in u_forward():
-                cp.wait_recv()
-
         def pick(values):
-            return jnp.where(b == 0, values[0], jnp.where(b == 1, values[1], jnp.where(b == 2, values[2], values[3])))
-
-        first = pick((0, 0, 0, 1))
-        parts = (
-            (pick((t, tm, um, um)), first),
-            (pick((t, tm, up, up)), pick((1, 1, 0, 1))),
-            (pick((tx, tp, t2, u2)), 0),
-            (pick((tx, tp, t2, u2)), 1),
-        )
+            return jnp.where(b == 0, values[0], jnp.where(b == 1, values[1], values[2]))
+
+        parts = [
+            (pick((t, tm, um)), 0),
+            (pick((t, tm, up)), pick((1, 1, 0))),
+            (pick((tx, tp, t2)), 0),
+            (pick((tx, tp, t2)), 1),
+        ]
+        compute(parts, 4 * b)
+        return 0
+
+    def compute(parts, first):
         parts = [(tt, half, pl.ds(pl.multiple_of(half * HALF, HALF), HALF)) for tt, half in parts]
         rows = jnp.concatenate([x[tt, rr, :] for tt, half, rr in parts], axis=0)
         for n in range(3):
@@ -281,20 +290,29 @@
             for i, (tt, half, rr) in enumerate(parts):
                 ctx[tt, rr, cols] = part[i * HALF:(i + 1) * HALF]
         for i, (tt, half, rr) in enumerate(parts):
-            kv_copy(tt, half, 4 * b + i).start()
+            kv_copy(tt, half, first + i).start()
         part = jnp.dot(rows, w[:, :GROUP], preferred_element_type=F32).astype(BF16)
         for i, (tt, half, rr) in enumerate(parts):
             q[tt, rr, :] = part[i * HALF:(i + 1) * HALF]
-        return 0
 
     u_yp[0].wait_recv()
     u_ym[0].wait_recv()
     for cp in u_forward():
         cp.start()
-    lax.fori_loop(0, 4, project, 0)
-
-    lat_copy = copy(lat, lat_prev, LAT, NX)
-    lat_copy.start()
+
+    @pl.when(c == 1)
+    def _():
+        for d in (1, 3, 2):
+            lat_copy(d).start()
+
+    lax.fori_loop(0, 3, project, 0)
+    u_yp[1].wait_recv()
+    u_ym[1].wait_recv()
+    u_x.wait_recv()
+    compute([(um, 1), (up, 1), (u2, 1)], 12)
+    for cp in u_forward():
+        cp.wait_recv()
+    compute([(u2, 0)], 15)
 
     for k in range(16):
         kv_copy(t, 0, k).wait_recv()
@@ -307,9 +325,6 @@
             o_copy(onward, CO, z + dz).start()
 
     scale = 1.0 / math.sqrt(HD)
-
-    def owner(j):
-        return (y + 1 + j) % 4
 
     def tile_at(yt, second_half):
         return 2 * (yt % 4) + jnp.where(second_half, here, 1 - here)
@@ -337,58 +352,54 @@
                 ok = ok & (listed[e] != listed[j])
             valid.append(ok)
         outs = []
+        ones = jnp.ones((4 * BLK, HD), BF16)
         for head in range(3):
             hc = slice(head * HD, (head + 1) * HD)
             vc = slice(GROUP + head * HD, GROUP + (head + 1) * HD)
             keys = jnp.concatenate([ctx[listed[j], :, hc] for j in range(4)], axis=0)
-            scores = lax.dot_general(q[i, :, hc], keys, (((1,), (1,)), ((), ())), preferred_element_type=F32) * scale
+            scores = lax.dot_general(q[i, :, hc], keys, (((1,), (1,)), ((), ())), preferred_element_type=F32)
             scores = [jnp.where(valid[j], scores[:, j * BLK:(j + 1) * BLK], -1e30) for j in range(4)]
             top = jnp.maximum(jnp.maximum(scores[0], scores[1]), jnp.maximum(scores[2], scores[3]))
             top = jnp.max(top, axis=1, keepdims=True)
-            expo = [jnp.exp(sc - top) for sc in scores]
-            total = jnp.sum((expo[0] + expo[1]) + (expo[2] + expo[3]), axis=1, keepdims=True)
-            probs = jnp.concatenate([(e / total).astype(BF16) for e in expo], axis=1)
+            probs = jnp.concatenate([jnp.exp((sc - top) * scale).astype(BF16) for sc in scores], axis=1)
             values = jnp.concatenate([ctx[listed[j], :, vc] for j in range(4)], axis=0)
-            outs.append(jnp.dot(probs, values, preferred_element_type=F32).astype(BF16))
+            sums = jnp.dot(probs, jnp.concatenate([values, ones], axis=1), preferred_element_type=F32)
+            outs.append((sums[:, :HD] / sums[:, HD:]).astype(BF16))
         att[i, :, lanes(y)] = jnp.concatenate(outs, axis=1)
 
-    def forward(k, late):
-        j = at(k, FORWARD)
+    def onward_p(j, late):
         a_copy(j, late, A_YP).wait_recv()
         a_copy(j, late, A_FP).start()
+
+    def onward_m(j, late):
         a_copy(j, late, A_YM).wait_recv()
         a_copy(j, late, A_FM).start()
 
     def attention(k, _):
         late = k >= 4
-        j = at(k % 4, ORDER)
-        attend(tile_at(y + 1 + j, late))
+        attend(tile_at(y + 1 + at(k % 4, ORDER), late))
 
         @pl.when(k == 0)
-        def _():
-            a_copy(3, False, A_YM).start()
-
-        @pl.when(k == 1)
-        def _():
-            a_copy(1, False, A_YP).start()
-
-        @pl.when(k == 2)
         def _():
             a_copy(2, False, A_YP).start()
             a_copy(2, False, A_YM).start()
 
-        @pl.when(k == 3)
-        def _():
+        @pl.when(k == 1)
+        def _():
+            a_copy(1, False, A_YP).start()
+
+        @pl.when(k == 2)
+        def _():
+            a_copy(3, False, A_YM).start()
+
+        @pl.when(k == 5)
+        def _():
+            onward_p(2, False)
+            onward_m(2, False)
+            a_copy(3, False, A_YP).start()
             a_copy(0, False, A_YM).start()
-            a_copy(3, False, A_YP).start()
+            a_copy(0, False, A_YP).start()
             a_copy(1, False, A_YM).start()
-            a_copy(0, False, A_YP).start()
-
-        @pl.when(late)
-        def _():
-            a_copy(j, True, A_YP).start()
-            a_copy(j, True, A_YM).start()
-            forward(k - 4, False)
 
         return 0
 
@@ -417,13 +428,44 @@
     def p_copy(p):
         return copy(psend.at[p], precv.at[p], P_X + p, XL)
 
-    def foreign(p, _):
-        psend[p] = product(p, False).astype(BF16)
+    def foreign(p):
+        mine = product(p, False)
+
+        @pl.when(c == 0)
+        def _():
+            psend[p] = mine.astype(BF16)
+
+        @pl.when(c == 1)
+        def _():
+            psend[p] = (mine + latr[(y + 1 + p) % 4].astype(F32)).astype(BF16)
+
         p_copy(p).start()
-        forward(p, True)
-        return 0
-
-    lax.fori_loop(0, 4, foreign, 0)
+
+    def late_sends(*tiles):
+        for j in tiles:
+            a_copy(j, True, A_YP).start()
+            a_copy(j, True, A_YM).start()
+
+    @pl.when(c == 1)
+    def _():
+        for d in (1, 2, 3):
+            lat_copy(d).wait_recv()
+
+    onward_p(1, False)
+    onward_m(3, False)
+    foreign(0)
+    onward_p(3, False)
+    onward_m(0, False)
+    late_sends(2, 1)
+    foreign(1)
+    onward_p(0, False)
+    onward_m(1, False)
+    late_sends(3, 0)
+    foreign(2)
+    foreign(3)
+    for j in ORDER:
+        onward_p(j, True)
+        onward_m(j, True)
 
     def s_copy(p):
         return copy(ssend.at[p], branch.at[y], S_Y + p, (NX[0], tok(y + 1 + p, here)))
@@ -453,7 +495,16 @@
     for p in range(4):
         p_copy(p).wait_send()
         s_copy(p).wait_send()
-    lat_copy.wait_send()
+
+    @pl.when(c == 0)
+    def _():
+        copy(lat, lat_prev, LAT, NX).wait_send()
+
+    @pl.when(c == 1)
+    def _():
+        for d in (1, 2, 3):
+            lat_copy(d).wait_send()
+
 
     @pl.when(jnp.logical_not(gather))
     def _():
@@ -468,16 +519,22 @@
         for name in ("o_zp", "o_zm", "o_z2") + CORE:
             o_copy(name, CO, z).wait_send()
 
-    lat_copy.wait_recv()
+
+    @pl.when(c == 1)
+    def _():
+        copy(lat, lat_prev, LAT, NX).wait_recv()
+
     for p in range(4):
         s_copy(p).wait_recv()
 
 
 def residual(branch, lat, out):
+    add = lax.axis_index("slot") % 2 == 1
     for zz in range(4):
         cols = slice(zz * COLS, (zz + 1) * COLS)
         pieces = [branch[yy, :, zz * PIECE:(zz + 1) * PIECE] for yy in range(4)]
-        out[:, cols] = (lat[:, cols].astype(F32) + jnp.concatenate(pieces, axis=1).astype(F32)).astype(BF16)
+        base = jnp.where(add, lat[:, cols].astype(F32), 0.0)
+        out[:, cols] = (base + jnp.concatenate(pieces, axis=1).astype(F32)).astype(BF16)
 
 
 def body(latents, gain, mod_table, slot_noise_level, key_block_index, counts, w_qkv, w_out):
@@ -501,6 +558,8 @@
             blocks,
             blocks,
             blocks,
+            blocks,
+            blocks,
             pltpu.SemaphoreType.DMA((4,)),
             pltpu.SemaphoreType.DMA((N_SEM,)),
             pltpu.SemaphoreType.DMA((N_SEM,)),

time: 157 us -> 155 us (0.987); the launches traced: 155 us -> 155 us
  no operation moved by 1% of the time
where the time goes in v4:
time: 155 us
  Pallas kernels  155 us (100%)
    pallas_call x1, Pallas kernels, body(): pl.pallas_call(kernel, out_shape=[jax.ShapeDtypeStruct((4, ROWS, COLS), B...  152 us

profile of v4, /device:TPU:1, one launch (start us, length us, event | category | flops | bytes accessed | tf_op | source)
XLA Modules:
  0.0 155.2 jit_solution(10543201598203540043)
XLA Ops:
  0.7 151.8 %window.1 = (bf16[4,128,1280]{2,1,0:T(8,128)(2,1)}, bf16[128,5120]{1,0:T(8,128)(2,1)}) custom-call(bf16[128,5120]{1,0:T(8,128)(2,1)} %bitcast.8, f32[1,5120]{1,0:T(1,128)} %bitcast.10, f32[16,2,5120]{2,1,0:T(2,128)} %mod.1, s32[1]{0:T(128)S(6)} %copy.9.level, s32[4,8]{1,0:T(4,128)} %bitcast.11, s32[8]{0:T(128)} %bitcast.12, bf16[3,320,384]{2,1,0:T(8,128)(2,1)} %wq.1, ...), custom_call_target="tpu_custom_call" | custom-call | tf_op jit(solution)/shard_map/window/pallas_call | solution.py:545
  152.5 2.8 %residual.1 = bf16[128,5120]{1,0:T(8,128)(2,1)} custom-call(bf16[4,128,1280]{2,1,0:T(8,128)(2,1)} %get-tuple-element.7.branch, bf16[128,5120]{1,0:T(8,128)(2,1)} %get-tuple-element.8.lat), custom_call_target="tpu_custom_call" | custom-call | tf_op jit(solution)/shard_map/residual/pallas_call | solution.py:572

commit v5 on v4

--- a/solution.py
+++ b/solution.py
@@ -43,8 +43,8 @@
 ORDER = (2, 1, 3, 0)
 
 
-def kernel(lat, gain, mod, level, ids, counts, wq, wo, branch, lat_prev,
-           x, w, wot, wout, q, ctx, att, psend, precv, ssend, latc, latr, local, ss, rs):
+def kernel(lat_in, gain, mod_in, level, ids, counts, wq, wo, branch, lat_prev,
+           x, w, wot, wout, q, ctx, att, psend, precv, ssend, latc, latr, lat, mod, local, go, ss, rs):
     s, t = lax.axis_index("slot"), lax.axis_index("tok")
     z, h, c = s // 4, (s // 2) % 2, s % 2
     y, l = t // 2, t % 2
@@ -75,6 +75,9 @@
         sent.append(cp)
         return cp
 
+    inputs = [pltpu.make_async_copy(lat_in, lat, local.at[4]), pltpu.make_async_copy(mod_in, mod, local.at[5])]
+    for cp in inputs:
+        cp.start()
     barrier = pltpu.get_barrier_semaphore()
     here, before = (l + c) % 2, (l + 1 - c) % 2
     peers = [XL, YP, YM, Y2, ZP, ZM, XH, CO, NX, PV]
@@ -93,6 +96,8 @@
     ]
     for cp in own:
         cp.start()
+    for cp in inputs:
+        cp.wait()
     lv = level[0]
     factor = gain[...] * (1.0 + mod[lv, 0:1, :])
     offset = mod[lv, 1:2, :]
@@ -152,9 +157,20 @@
     for half in range(2):
         if half == 1:
             lax.fori_loop(4, 8, norm, 0)
+        if half == 0:
+            t_x.append(send(shard(t, half), "t_x%d" % half, XL))
+
+            @pl.when(c == 0)
+            def _():
+                pl.semaphore_wait(go, 1)
+
         t_yp.append(send(shard(t, half), "t_yp%d" % half, YP))
         t_ym.append(send(shard(t, half), "t_ym%d" % half, YM))
-        t_x.append(send(shard(t, half), "t_x%d" % half, XL))
+
+    @pl.when(c == 1)
+    def _():
+        t_yp[0].wait_send()
+        pl.semaphore_signal(go, inc=1, device_id=CO, device_id_type=MESH)
 
     @pl.when(c == 0)
     def _():
@@ -183,6 +199,7 @@
             copy(src, src, SEM["o_a0"] + d, YP).wait_recv()
         o_copy("o_xh", XH, z).start()
 
+    t_x.append(send(shard(t, 1), "t_x1", XL))
     t_yp[0].wait_recv()
     t_fp = send(shard(tm, 0), "t_fp", YP)
     w_zp0.wait_recv()
@@ -480,7 +497,13 @@
     lax.fori_loop(0, 4, finish, 0)
 
     for cp in sent:
-        cp.wait_send()
+        if cp is not t_yp[0]:
+            cp.wait_send()
+
+    @pl.when(c == 0)
+    def _():
+        t_yp[0].wait_send()
+
     for cp in u_forward():
         cp.wait_send()
 
@@ -545,7 +568,7 @@
     branch, lat_prev = pl.pallas_call(
         kernel,
         out_shape=[jax.ShapeDtypeStruct((4, ROWS, COLS), BF16), jax.ShapeDtypeStruct((ROWS, D), BF16)],
-        in_specs=[vmem, vmem, vmem, smem, smem, smem, hbm, hbm],
+        in_specs=[hbm, vmem, hbm, smem, smem, smem, hbm, hbm],
         out_specs=[hbm, hbm],
         scratch_shapes=[
             pltpu.VMEM((8, ROWS, D), BF16),
@@ -560,7 +583,10 @@
             blocks,
             blocks,
             blocks,
-            pltpu.SemaphoreType.DMA((4,)),
+            pltpu.VMEM((ROWS, D), BF16),
+            pltpu.VMEM((16, 2, D), F32),
+            pltpu.SemaphoreType.DMA((6,)),
+            pltpu.SemaphoreType.REGULAR,
             pltpu.SemaphoreType.DMA((N_SEM,)),
             pltpu.SemaphoreType.DMA((N_SEM,)),
         ],

time: 155 us -> 154 us (level)
  Pallas kernels: 155 us -> 153 us
where the time goes in v5:
time: 154 us
  Pallas kernels  153 us (99%)
    pallas_call x1, Pallas kernels, body(): pl.pallas_call(kernel, out_shape=[jax.ShapeDtypeStruct((4, ROWS, COLS), B...  150 us

profile of v5, /device:TPU:1, one launch (start us, length us, event | category | flops | bytes accessed | tf_op | source)
XLA Modules:
  0.0 153.7 jit_solution(9699676169049077354)
XLA Ops:
  0.7 150.3 %window.1 = (bf16[4,128,1280]{2,1,0:T(8,128)(2,1)}, bf16[128,5120]{1,0:T(8,128)(2,1)}) custom-call(bf16[128,5120]{1,0:T(8,128)(2,1)} %bitcast.8, f32[1,5120]{1,0:T(1,128)} %bitcast.10, f32[16,2,5120]{2,1,0:T(2,128)} %mod_in.1, s32[1]{0:T(128)S(6)} %copy.9.level, s32[4,8]{1,0:T(4,128)} %bitcast.11, s32[8]{0:T(128)} %bitcast.12, bf16[3,320,384]{2,1,0:T(8,128)(2,1)} %wq.1, ...), custom_call_target="tpu_custom_call" | custom-call | tf_op jit(solution)/shard_map/window/pallas_call | solution.py:568
  151.0 2.8 %residual.1 = bf16[128,5120]{1,0:T(8,128)(2,1)} custom-call(bf16[4,128,1280]{2,1,0:T(8,128)(2,1)} %get-tuple-element.7.branch, bf16[128,5120]{1,0:T(8,128)(2,1)} %get-tuple-element.8.lat), custom_call_target="tpu_custom_call" | custom-call | tf_op jit(solution)/shard_map/residual/pallas_call | solution.py:598

commit v6 on v5

--- a/solution.py
+++ b/solution.py
@@ -278,6 +278,7 @@
             def _():
                 o_copy("o_zm", ZM, z + 1).wait_recv()
                 o_copy("o_z2", ZM, z + 1).start()
+                o_copy("o_co2", CO, z + 1).start()
 
             t_yp[1].wait_recv()
             t_ym[0].wait_recv()
@@ -331,15 +332,15 @@
         cp.wait_recv()
     compute([(u2, 0)], 15)
 
+    @pl.when(active)
+    def _():
+        for name, dz, onward in (("o_zp", 3, "o_co1"), ("o_z2", 2, "o_co3")):
+            o_copy(name, ZP, z + dz).wait_recv()
+            o_copy(onward, CO, z + dz).start()
+
     for k in range(16):
         kv_copy(t, 0, k).wait_recv()
 
-    @pl.when(active)
-    def _():
-        for name, dz, onward in (("o_zp", 3, "o_co1"), ("o_zm", 1, "o_co2"), ("o_z2", 2, "o_co3")):
-            if name != "o_zm":
-                o_copy(name, ZP, z + dz).wait_recv()
-            o_copy(onward, CO, z + dz).start()
 
     scale = 1.0 / math.sqrt(HD)
 

time: 154 us -> 155 us (level)
  no operation moved by 1% of the time
where the time goes in v6:
time: 155 us; the launch traced here: 154 us
  Pallas kernels  154 us (99%)
    pallas_call x1, Pallas kernels, body(): pl.pallas_call(kernel, out_shape=[jax.ShapeDtypeStruct((4, ROWS, COLS), B...  151 us

profile of v6, /device:TPU:1, one launch (start us, length us, event | category | flops | bytes accessed | tf_op | source)
XLA Modules:
  0.0 154.2 jit_solution(5862370264457022821)
XLA Ops:
  0.7 150.8 %window.1 = (bf16[4,128,1280]{2,1,0:T(8,128)(2,1)}, bf16[128,5120]{1,0:T(8,128)(2,1)}) custom-call(bf16[128,5120]{1,0:T(8,128)(2,1)} %bitcast.8, f32[1,5120]{1,0:T(1,128)} %bitcast.10, f32[16,2,5120]{2,1,0:T(2,128)} %mod_in.1, s32[1]{0:T(128)S(6)} %copy.9.level, s32[4,8]{1,0:T(4,128)} %bitcast.11, s32[8]{0:T(128)} %bitcast.12, bf16[3,320,384]{2,1,0:T(8,128)(2,1)} %wq.1, ...), custom_call_target="tpu_custom_call" | custom-call | tf_op jit(solution)/shard_map/window/pallas_call | solution.py:569
  151.5 2.8 %residual.1 = bf16[128,5120]{1,0:T(8,128)(2,1)} custom-call(bf16[4,128,1280]{2,1,0:T(8,128)(2,1)} %get-tuple-element.7.branch, bf16[128,5120]{1,0:T(8,128)(2,1)} %get-tuple-element.8.lat), custom_call_target="tpu_custom_call" | custom-call | tf_op jit(solution)/shard_map/residual/pallas_call | solution.py:599
